TPU v7x, 512 devices: a whole 4x8x8 slice. The times are simulated.
512 devices in a mesh: kvh: 8 (over x, core), ctx: 64 (over y, z).
Axes of the slice: x: 4, y: 8, z: 8, core: 2. Of those that a mesh axis runs over, the one named last changes fastest.
Arguments:
- queries: bfloat16 [128, 8192], P(None, 'kvh'), may hold values from -130 to 130
- cache_keys: bfloat16 [65536, 1024], P('ctx', 'kvh'), may hold values from -6 to 6
- cache_values: bfloat16 [65536, 1024], P('ctx', 'kvh'), may hold values from -6 to 6
- lengths: int32 [64], P('ctx'), may hold values from 2 to 1024, as said below
- w_out: bfloat16 [8192, 8192], P('kvh', 'ctx'), may hold values from -0.0625 to 0.0625
Outputs:
- mixed: bfloat16 [128, 8192], P('kvh', 'ctx')
Inputs may be any that keep to these rules, and one draw needn't show every extreme that they name: `lengths`: the number of valid positions at the start of each segment of 1024 positions; at least one segment is full.
All inputs are finite; a program needn't handle non-finite values.
Results may differ from a plain program's by a relative error of at most 0.005.
Values may be sent and summed in bfloat16 or wider, within the bound.
A program may use at most 192 MiB of HBM per device.

v0:
```python
import math

import jax
import jax.numpy as jnp
from jax import lax
from jax.sharding import PartitionSpec as P

HEADS = 64
KVH = 8
HD = 128


def local_partials(queries, cache_keys, cache_values, lengths):
    score_scale = 1.0 / math.sqrt(HD)
    row_count = queries.shape[0]
    per_group = HEADS // KVH
    head_block = min(per_group, max(1, 512 // row_count))
    valid_mask = lax.iota(jnp.int32, cache_keys.shape[0]) < lengths[0]
    maxima_list = []
    totals_list = []
    outputs_list = []
    for first_head in range(0, per_group, head_block):
        column = first_head * HD
        query_block = queries[:, column : column + head_block * HD].reshape(
            row_count, head_block, HD
        )
        scores = (
            jnp.einsum("qhd,kd->hqk", query_block, cache_keys, preferred_element_type=jnp.float32)
            * score_scale
        )
        scores = jnp.where(valid_mask[None, None, :], scores, -jnp.inf)
        peak_row = jnp.max(scores, axis=-1)
        weights = jnp.exp(scores - peak_row[:, :, None])
        totals_list.append(jnp.sum(weights, axis=-1))
        maxima_list.append(peak_row)
        outputs_list.append(
            jnp.einsum(
                "hqk,kd->qhd",
                weights.astype(jnp.bfloat16),
                cache_values,
                preferred_element_type=jnp.float32,
            )
        )
    return (
        jnp.concatenate(maxima_list, axis=0),
        jnp.concatenate(totals_list, axis=0),
        jnp.concatenate(outputs_list, axis=1),
    )


def shards(queries, cache_keys, cache_values, lengths, w_out):
    maxima, totals, outputs = local_partials(queries, cache_keys, cache_values, lengths)
    row_count = outputs.shape[0]
    head_count = outputs.shape[1]
    joined = lax.pmax(maxima, "ctx")
    factor = jnp.exp(maxima - joined)
    denom, numer = lax.psum((totals * factor, outputs * factor.T[:, :, None]), "ctx")
    attended = (
        (numer / denom.T[:, :, None]).reshape(row_count, head_count * HD).astype(jnp.bfloat16)
    )
    mixed = lax.psum_scatter(
        jnp.dot(attended, w_out, preferred_element_type=jnp.float32),
        "kvh",
        scatter_dimension=0,
        tiled=True,
    )
    return mixed.astype(jnp.bfloat16)


def solution(mesh):
    in_specs = (P(None, "kvh"), P("ctx", "kvh"), P("ctx", "kvh"), P("ctx"), P("kvh", "ctx"))
    out_specs = P("kvh", "ctx")
    return jax.shard_map(shards, mesh=mesh, in_specs=in_specs, out_specs=out_specs, check_vma=False)
```

profile of v0, /device:TPU:1, one launch (start us, length us, event | category | flops | bytes accessed | tf_op | source)
XLA Modules:
  0.0 355.1 jit_solution(10503697270766560614)
XLA Ops:
  6.5 0.0 copy-start
  7.2 1.0 fusion.26
  8.2 0.1 copy.19
  8.4 0.1 copy.20
  8.5 0.4 bitcast_reduce_fusion.1
  8.9 0.8 fusion.2
  9.7 0.0 copy-start.2
  9.7 0.5 fusion.4
  10.3 0.4 copy-done.2
  10.7 0.8 convolution_bitcast_fusion
  11.5 0.8 convolution_bitcast_fusion.1
  12.3 0.0 copy-start.1
  12.4 123.3 %pmax.7 = f32[8,128]{1,0:T(8,128)S(1)} all-reduce(f32[8,128]{1,0:T(8,128)S(1)} %pad_maximum_fusion), channel_id=1, replica_groups=mesh['kvh'=8,'ctx'=64] {'ctx'}, use_global_device_ids=true, to_apply=%region_2.3 | all-reduce | flops 1024 | bytes 8192 | tf_op jit(solution)/shard_map/pmax | solution.py:55
  135.7 1.0 maximum_multiply_fusion
  136.7 0.0 all-reduce.2.cloned.1.call-update
  136.7 0.0 reduce-scatter.2.cloned.1.call-start
  136.7 110.5 %psum.15 = f32[128,8]{0,1:T(8,128)S(1)} all-reduce(f32[128,8]{0,1:T(8,128)S(1)} %get-tuple-element.9), channel_id=1, replica_groups=mesh['kvh'=8,'ctx'=64] {'ctx'}, use_global_device_ids=true, to_apply=%region_6.7 | all-reduce | flops 1024 | bytes 8192 | tf_op jit(solution)/shard_map/psum | solution.py:57
  247.2 62.0 %all-reduce.2.cloned.1.call-done = f32[128,8,128]{2,0,1:T(8,128)} async-done(((f32[128,8,128]{2,0,1:T(8,128)}), f32[128,8,128]{2,0,1:T(8,128)}) %all-reduce.2.cloned.1.call-update) | async-done | bytes 524304 | tf_op jit(solution)/shard_map/psum | solution.py:57
  309.3 1.2 divide_convert_fusion
  310.5 0.2 copy.14
  310.7 0.9 fusion.27
  311.6 0.0 reduce-scatter.2.cloned.1.call-update
  311.6 35.3 %reduce-scatter.2.cloned.1.call-done = f32[16,128]{1,0:T(8,128)} async-done(((f32[128,128]{1,0:T(8,128)}), f32[16,128]{1,0:T(8,128)}) %reduce-scatter.2.cloned.1.call-update) | async-done | bytes 8208 | tf_op jit(solution)/shard_map/reduce_scatter | solution.py:61
  346.9 1.3 convert_element_type.19
  (6 shorter events, 0.0 us)
Async XLA Ops:
  6.5 2.0 copy-start
  6.5 302.7 %all-reduce.2.cloned.1.call-start = ((), (), s32[]{:S(2)}) async-start(), calls=%async_computation.1 | async-start | bytes 1048576 | tf_op jit(solution)/shard_map/psum | solution.py:57
  9.7 1.0 copy-start.2
  12.3 298.4 %copy-start.1 = (bf16[1024,128]{1,0:T(8,128)(2,1)S(1)}, bf16[1024,128]{1,0:T(8,128)(2,1)}, u32[]{:S(2)}) copy-start(bf16[1024,128]{1,0:T(8,128)(2,1)} %param.9) | copy-start | bytes 786436
  136.7 210.2 %reduce-scatter.2.cloned.1.call-start = ((), (), s32[]{:S(2)}) async-start(), calls=%async_computation.2 | async-start | bytes 73728 | tf_op jit(solution)/shard_map/reduce_scatter | solution.py:61
Sparse Core Ops, SparseCore 0:
  136.8 172.4 all-reduce.1
  312.3 34.6 reduce-scatter.1
where the time goes:
time: 356 us; the launch traced here: 355 us
  blocking collectives  234 us (66%)
  waiting for transfers between devices  97.4 us (27%)
  between operations  14.2 us (4%)
  other arithmetic  4.09 us (1%)
  matrix products  3.77 us (1%)
    pmax x1, blocking collectives, shards(): joined = lax.pmax(maxima, 'ctx')  123 us
    psum x1, blocking collectives, shards(): lax.psum((totals * factor, outputs * factor.T[:, :, None]), 'ctx')  110 us
    psum x1, waiting for transfers between devices, shards(): lax.psum((totals * factor, outputs * factor.T[:, :, None]), 'ctx')  62 us
    reduce_scatter x1, waiting for transfers between devices, shards(): lax.psum_scatter(jnp.dot(attended, w_out, preferred_element_type=jnp.floa...  35.3 us
  transfers between devices with their start and end apart: 2, of which 2 were waited for; matrix products, arithmetic and copies ran while one was open for 0% of the time, Pallas kernels for 0%

commit v1 on v0

v1 whole, which is shorter than its diff:
```python
import functools
import math

import jax
import jax.numpy as jnp
from jax import lax
from jax.experimental import pallas as pl
from jax.experimental.pallas import tpu as pltpu
from jax.sharding import PartitionSpec as P

HD = 128
HALF = HD // 2
STAT_ROWS = 16
MASKED = -1e30
SCALE = 1.0 / math.sqrt(HD)
LOG2E = math.log2(math.e)
MESH = pl.DeviceIdType.MESH


def ceil_to(value, unit):
    return -(-value // unit) * unit


def split_rows(stat, rows):
    high = stat.astype(jnp.bfloat16).astype(jnp.float32)
    rest = stat - high
    middle = rest.astype(jnp.bfloat16).astype(jnp.float32)
    low = rest - middle
    row = lax.broadcasted_iota(jnp.int32, (rows, stat.shape[1]), 0)
    return jnp.where(
        row == 0, high, jnp.where(row == 1, middle, jnp.where(row == 2, low, 0.0))
    )


def join_rows(rows):
    return rows[0:1] + rows[1:2] + rows[2:3]


def merge(parts, stats):
    top = functools.reduce(jnp.maximum, stats)
    shares = [jnp.exp(stat - top) for stat in stats]
    total = functools.reduce(jnp.add, shares)
    merged = functools.reduce(
        jnp.add, [part * share for part, share in zip(parts, shares)]
    )
    return merged / total, top + jnp.log(total)


def kernel(
    nk, n,
    len_hbm, q_hbm, k_hbm, v_hbm, w_hbm, out_ref,
    len_ref, q_ref, k_ref, v_ref, w_ref, vt_ref, wt_ref,
    send1, recv1, send2, recv2, att, send3, recv3,
    load_sem, send_sem, recv_sem,
):
    rows = q_ref.shape[0]
    keys = k_ref.shape[0]
    share = HALF // n
    kvh = lax.axis_index("kvh")
    ctx = lax.axis_index("ctx")
    y, z = ctx // n, lax.rem(ctx, n)

    loads = [
        pltpu.make_async_copy(q_hbm, q_ref, load_sem.at[0]),
        pltpu.make_async_copy(k_hbm, k_ref.at[:, pl.ds(0, HD)], load_sem.at[1]),
        pltpu.make_async_copy(v_hbm, v_ref, load_sem.at[2]),
        pltpu.make_async_copy(w_hbm, w_ref, load_sem.at[3]),
        pltpu.make_async_copy(len_hbm, len_ref, load_sem.at[4]),
    ]
    for load in loads:
        load.start()

    def on_y(step):
        return (kvh, lax.rem(y + step, n) * n + z)

    def on_z(step):
        return (kvh, y * n + lax.rem(z + step, n))

    def on_kvh(step):
        return (lax.rem(kvh + step, nk), ctx)

    barrier = pltpu.get_barrier_semaphore()
    for step in range(1, n):
        pl.semaphore_signal(barrier, inc=1, device_id=on_y(step), device_id_type=MESH)
        pl.semaphore_signal(barrier, inc=1, device_id=on_z(step), device_id_type=MESH)
    for step in range(1, nk):
        pl.semaphore_signal(barrier, inc=1, device_id=on_kvh(step), device_id_type=MESH)

    def send(src, dst, index, device):
        pltpu.make_async_remote_copy(
            src_ref=src, dst_ref=dst, send_sem=send_sem.at[index],
            recv_sem=recv_sem.at[index], device_id=device, device_id_type=MESH,
        ).start()

    def take(ref, sem):
        pltpu.make_async_copy(ref, ref, sem).wait()

    loads[4].wait()
    position = lax.broadcasted_iota(jnp.int32, (keys, HD), 0)
    column = lax.broadcasted_iota(jnp.int32, (keys, HD), 1)
    bias = jnp.where((column == 0) & (position >= len_ref[0]), MASKED, 0.0)
    k_ref[:, HD:] = bias.astype(jnp.bfloat16)
    lane = lax.broadcasted_iota(jnp.int32, (2 * rows, HD), 1)
    unit = jnp.where(lane == 0, 1.0, 0.0).astype(jnp.bfloat16)

    loads[2].wait()
    vt_ref[:HD] = v_ref[...].T
    vt_ref[HD:] = jnp.ones((STAT_ROWS, keys), jnp.bfloat16)
    loads[0].wait()
    loads[1].wait()
    pl.semaphore_wait(barrier, 2 * (n - 1) + nk - 1)

    for pair in range(n // 2):
        heads = [lax.rem(y + 1 + 2 * pair, n), lax.rem(y + 2 + 2 * pair, n)]
        query = jnp.concatenate(
            [q_ref[:, pl.ds(pl.multiple_of(h * HD, HD), HD)] for h in heads], axis=0
        )
        query = jnp.concatenate([query, unit], axis=1)
        scores = lax.dot_general(
            k_ref[...], query, (((1,), (1,)), ((), ())),
            preferred_element_type=jnp.float32,
        )
        peak = jnp.max(scores, axis=0, keepdims=True)
        weights = jnp.exp2((scores - peak) * (SCALE * LOG2E)).astype(jnp.bfloat16)
        outs = jnp.dot(vt_ref[...], weights, preferred_element_type=jnp.float32)
        total = outs[HD : HD + 1]
        stat = peak * SCALE + jnp.log(total)
        outs = (outs[:HD] / total).astype(jnp.bfloat16)
        tail = split_rows(stat, STAT_ROWS).astype(jnp.bfloat16)
        for slot, h in enumerate(heads):
            here = slice(slot * rows, (slot + 1) * rows)
            own = pair == n // 2 - 1 and slot == 1
            first = recv1.at[0, y] if own else send1.at[0, h]
            first[:HALF] = outs[:HALF, here]
            first[HALF:] = tail[:, here]
            if not own:
                send(first, recv1.at[0, y], 0, (kvh, h * n + z))
            second = send1.at[1, h]
            second[:HALF] = outs[HALF:, here]
            second[HALF:] = tail[:, here]

            @pl.when(h != z)
            def _():
                send(second, recv1.at[1, z], 1, (kvh, y * n + h))

            @pl.when(h == z)
            def _():
                recv1[1, z, :HALF] = outs[HALF:, here]
                recv1[1, z, HALF:] = tail[:, here]

    loads[3].wait()
    for kind in range(2):
        for major in range(n):
            blocks = []
            for minor in range(n // 2):
                other = 2 * minor + (major + kind) % 2
                by, bz = (major, other) if kind == 0 else (other, major)
                for start in (by * HD + bz * share, bz * HD + HALF + by * share):
                    blocks.append(w_ref[start : start + share].astype(jnp.float32))
            block = jnp.concatenate(blocks, axis=0)
            at = (kind * n + major) * HALF
            wt_ref[:, at : at + HALF] = block.T.astype(jnp.bfloat16)

    message = send2.shape[2]
    mine = (y, z)
    for kind in range(2):
        take(recv1.at[kind, pl.ds(0, n - 1)], recv_sem.at[kind])
        merged, stat = merge(
            [recv1[kind, j, :HALF].astype(jnp.float32) for j in range(n)],
            [join_rows(recv1[kind, j, HALF:].astype(jnp.float32)) for j in range(n)],
        )
        tail = split_rows(stat, message - share)
        for j in range(n):
            piece = jnp.concatenate([merged[j * share : (j + 1) * share], tail], axis=0)
            send2[kind, j] = piece.astype(jnp.bfloat16)
        across = mine[1 - kind]
        recv2[kind, across] = send2[kind, across]
        for step in range(1, n):
            to = lax.rem(across + step, n)
            device = (kvh, y * n + to) if kind == 0 else (kvh, to * n + z)
            send(send2.at[kind, to], recv2.at[kind, across], 2 + kind, device)

    pieces = []
    for kind in range(2):
        take(recv2.at[kind, pl.ds(0, n - 1)], recv_sem.at[2 + kind])
        merged, _ = merge(
            [recv2[kind, j, :share].astype(jnp.float32) for j in range(n)],
            [
                join_rows(recv2[kind, j, share:].astype(jnp.float32))
                for j in range(n)
            ],
        )
        pieces.append(merged)
    parity = lax.rem(y + z, 2)
    major = y + parity * (z - y)
    minor = (z + parity * (y - z)) // 2
    att[parity, major, minor] = jnp.concatenate(pieces, axis=0).astype(jnp.bfloat16)

    for step in range(1, n):
        to = lax.rem(y + parity * step, n) * n + lax.rem(z + (1 - parity) * step, n)
        tile = att.at[parity, major, minor]
        send(tile, tile, 4, (kvh, to))
    tiles = att.at[0, pl.ds(0, n - 1), 0]
    take(tiles, recv_sem.at[4])
    for step in range(1, n):
        send(att.at[0, y], att.at[0, y], 5, on_y(step))
        send(att.at[1, z], att.at[1, z], 6, on_z(step))
    take(att.at[0, pl.ds(0, n - 1)], recv_sem.at[5])
    take(att.at[1, pl.ds(0, n - 1)], recv_sem.at[6])

    features = att[...].reshape(n * HD, rows)
    mixed = jnp.dot(wt_ref[...], features, preferred_element_type=jnp.float32).T
    send3[...] = mixed.reshape(send3.shape)
    for step in range(1, nk):
        to = lax.rem(kvh + step, nk)
        send(send3.at[to], recv3.at[kvh], 7, on_kvh(step))
    recv3[kvh] = send3[kvh]
    take(recv3.at[pl.ds(0, nk - 1)], recv_sem.at[7])
    out_ref[...] = jnp.sum(recv3[...], axis=0).astype(jnp.bfloat16)

    for kind in range(2):
        take(send1.at[kind, pl.ds(0, n - 1)], send_sem.at[kind])
        take(send2.at[kind, pl.ds(0, n - 1)], send_sem.at[2 + kind])
        take(att.at[kind, pl.ds(0, n - 1)], send_sem.at[5 + kind])
    take(tiles, send_sem.at[4])
    take(send3.at[pl.ds(0, nk - 1)], send_sem.at[7])


def solution(mesh):
    nk = mesh.shape["kvh"]
    n = math.isqrt(mesh.shape["ctx"])
    share = HALF // n
    message = ceil_to(share + 3, 16)

    def step(queries, cache_keys, cache_values, lengths, w_out):
        rows, keys = queries.shape[0], cache_keys.shape[0]
        bf16, f32 = jnp.bfloat16, jnp.float32
        anywhere = pl.BlockSpec(memory_space=pl.ANY)
        return pl.pallas_call(
            functools.partial(kernel, nk, n),
            out_shape=jax.ShapeDtypeStruct((rows // nk, HD), bf16),
            in_specs=[anywhere] * 5,
            out_specs=pl.BlockSpec(memory_space=pltpu.VMEM),
            scratch_shapes=[
                pltpu.SMEM((1,), jnp.int32),
                pltpu.VMEM(queries.shape, bf16),
                pltpu.VMEM((keys, 2 * HD), bf16),
                pltpu.VMEM((keys, HD), bf16),
                pltpu.VMEM(w_out.shape, bf16),
                pltpu.VMEM((HD + STAT_ROWS, keys), bf16),
                pltpu.VMEM((HD, n * HD), bf16),
                pltpu.VMEM((2, n, HALF + STAT_ROWS, rows), bf16),
                pltpu.VMEM((2, n, HALF + STAT_ROWS, rows), bf16),
                pltpu.VMEM((2, n, message, rows), bf16),
                pltpu.VMEM((2, n, message, rows), bf16),
                pltpu.VMEM((2, n, n // 2, 2 * share, rows), bf16),
                pltpu.VMEM((nk, rows // nk, HD), f32),
                pltpu.VMEM((nk, rows // nk, HD), f32),
                pltpu.SemaphoreType.DMA((5,)),
                pltpu.SemaphoreType.DMA((8,)),
                pltpu.SemaphoreType.DMA((8,)),
            ],
            compiler_params=pltpu.CompilerParams(
                collective_id=0, has_side_effects=True, vmem_limit_bytes=60 * 2**20
            ),
        )(lengths, queries, cache_keys, cache_values, w_out)

    in_specs = (P(None, "kvh"), P("ctx", "kvh"), P("ctx", "kvh"), P("ctx"), P("kvh", "ctx"))
    out_specs = P("kvh", "ctx")
    return jax.shard_map(step, mesh=mesh, in_specs=in_specs, out_specs=out_specs, check_vma=False)
```

time: 356 us -> 45.6 us (0.13)
  blocking collectives: 234 us -> 0 us
  waiting for transfers between devices: 97.4 us -> 0 us
  Pallas kernels: 0 us -> 43.5 us
  between operations: 14.2 us -> 0.66 us
  other arithmetic: 4.09 us -> 0 us
  matrix products: 3.77 us -> 0 us
    pmax x1 -> x0, blocking collectives: 123 us -> none  [shards(): joined = lax.pmax(maxima, 'ctx')]
    psum x1 -> x0, blocking collectives: 110 us -> none  [shards(): lax.psum((totals * factor, outputs * factor.T[:, :, None]), 'ctx')]
    psum x1 -> x0, waiting for transfers between devices: 62 us -> none  [shards(): lax.psum((totals * factor, outputs * factor.T[:, :, None]), 'ctx')]
    pallas_call x0 -> x1, Pallas kernels: none -> 43.5 us  [step(): pl.pallas_call(functools.partial(kernel, nk, n), out_shape=jax.ShapeDtype...]
    reduce_scatter x1 -> x0, waiting for transfers between devices: 35.3 us -> none  [shards(): lax.psum_scatter(jnp.dot(attended, w_out, preferred_element_type=jnp.floa...]
    dot_general x5 -> x0, matrix products: 3.77 us -> none  [the longest x2 1.67 us: local_partials(): jnp.einsum('hqk,kd->qhd', weights.astype(jnp.bfloat16), cache_values, pre...]
  transfers between devices with their start and end apart: 2 -> 0, of which waited for: 2 -> 0; matrix products, arithmetic and copies ran while one was open for 0% -> 0% of each run, Pallas kernels for 0% -> 0%
where the time goes in v1:
time: 45.6 us; the launch traced here: 45.4 us
  Pallas kernels  43.5 us (95%)
  local copies, waits for them, and re-layouts  1.28 us (3%)
  between operations  0.66 us (1%)
    pallas_call x1, Pallas kernels, step(): pl.pallas_call(functools.partial(kernel, nk, n), out_shape=jax.ShapeDtype...  43.5 us
    unnamed x1, local copies, waits for them, and re-layouts  1.28 us

profile of v1, /device:TPU:1, one launch (start us, length us, event | category | flops | bytes accessed | tf_op | source)
XLA Modules:
  0.0 45.4 jit_solution(14364418242006451414)
XLA Ops:
  0.7 43.5 %shard_map.55 = bf16[16,128]{1,0:T(8,128)(2,1)} custom-call(s32[1]{0:T(128)S(6)} %copy.7.len_hbm, bf16[128,1024]{1,0:T(8,128)(2,1)} %q_hbm.1, bf16[1024,128]{1,0:T(8,128)(2,1)} %k_hbm.1, bf16[1024,128]{1,0:T(8,128)(2,1)} %v_hbm.1, bf16[1024,128]{1,0:T(8,128)(2,1)} %w_hbm.1), custom_call_target="tpu_custom_call" | custom-call | tf_op jit(solution)/shard_map/pallas_call | solution.py:239
  44.1 1.3 %copy.8 = bf16[16,128]{1,0:T(8,128)(2,1)} copy(bf16[16,128]{1,0:T(8,128)(2,1)} %shard_map.55) | data formatting | bytes 8192

commit v2 on v0

v2 whole, which is shorter than its diff:
```python
import functools
import math

import jax
import jax.numpy as jnp
from jax import lax
from jax.experimental import pallas as pl
from jax.experimental.pallas import tpu as pltpu
from jax.sharding import PartitionSpec as P

HD = 128
HALF = HD // 2
ONE_ROWS = 16
VMEM_BYTES = 53 * 2**20 + 800 * 2**10
MASKED = -1e30
SCALE = 1.0 / math.sqrt(HD)
LOG2E = math.log2(math.e)
MESH = pl.DeviceIdType.MESH


def merge(parts, stats):
    top = functools.reduce(jnp.maximum, stats)
    shares = [jnp.exp(stat - top) for stat in stats]
    total = functools.reduce(jnp.add, shares)
    scale = 1.0 / total
    merged = functools.reduce(
        jnp.add, [part * (share * scale) for part, share in zip(parts, shares)]
    )
    return merged, top + jnp.log(total)


def far_first(n):
    return sorted(range(1, n), key=lambda step: -min(step, n - step))


def merge_slots(slots, stats):
    n = slots.shape[0]
    return merge(
        [slots[j].astype(jnp.float32) for j in range(n)], [stats[j] for j in range(n)]
    )


def kernel(
    nk, n,
    len_hbm, q_hbm, k_hbm, v_hbm, w_hbm, out_ref,
    len_ref, q_ref, k_ref, v_ref, w_ref, vt_ref, wt_ref, scores,
    send1, recv1, recv2, stat0, stat1, stat2, att, send3, recv3,
    load_sem, send_sem, recv_sem,
):
    rows = q_ref.shape[0]
    keys = k_ref.shape[0]
    pairs = n // 2
    kvh = lax.axis_index("kvh")
    ctx = lax.axis_index("ctx")
    y, z = ctx // n, lax.rem(ctx, n)
    mine = (y, z)

    load_k = pltpu.make_async_copy(k_hbm, k_ref.at[:, pl.ds(0, HD)], load_sem.at[0])
    load_q = pltpu.make_async_copy(q_hbm, q_ref, load_sem.at[1])
    load_len = pltpu.make_async_copy(len_hbm, len_ref, load_sem.at[2])
    load_v = pltpu.make_async_copy(v_hbm, v_ref, load_sem.at[3])
    load_w = pltpu.make_async_copy(w_hbm, w_ref, load_sem.at[4])
    load_k.start()
    load_q.start()
    load_len.start()

    def along(kind, to):
        return (kvh, to * n + z) if kind == 0 else (kvh, y * n + to)

    def on_kvh(step):
        return (lax.rem(kvh + step, nk), ctx)

    barrier = pltpu.get_barrier_semaphore()
    for step in far_first(n):
        for kind in range(2):
            device = along(kind, lax.rem(mine[kind] + step, n))
            pl.semaphore_signal(barrier, inc=1, device_id=device, device_id_type=MESH)
    for step in range(1, nk):
        pl.semaphore_signal(barrier, inc=1, device_id=on_kvh(step), device_id_type=MESH)

    load_v.start()
    load_w.start()

    def send(src, dst, index, device):
        pltpu.make_async_remote_copy(
            src_ref=src, dst_ref=dst, send_sem=send_sem.at[index],
            recv_sem=recv_sem.at[index], device_id=device, device_id_type=MESH,
        ).start()

    def take(ref, sem):
        pltpu.make_async_copy(ref, ref, sem).wait()

    lane = lax.broadcasted_iota(jnp.int32, (2 * rows, HD), 1)
    unit = jnp.where(lane == 0, 1.0, 0.0).astype(jnp.bfloat16)
    position = lax.broadcasted_iota(jnp.int32, (keys, HD), 0)
    column = lax.broadcasted_iota(jnp.int32, (keys, HD), 1)
    load_len.wait()
    bias = jnp.where((column == 0) & (position >= len_ref[0]), MASKED, 0.0)
    k_ref[:, HD:] = bias.astype(jnp.bfloat16)

    orders = [
        [lax.rem(mine[kind] // 2 + step, pairs) for step in far_first(pairs) + [0]]
        for kind in range(2)
    ]

    def give(kind, place, owner):
        device = along(kind, owner)
        send(send1.at[kind, owner], recv1.at[kind, mine[kind]], kind, device)
        send(stat0.at[kind, place], stat1.at[kind, mine[kind]], 7 + kind, device)

    def score(pair):
        heads = [orders[kind][pair] + kind * pairs for kind in range(2)]
        query = jnp.concatenate(
            [q_ref[:, pl.ds(pl.multiple_of(h * HD, HD), HD)] for h in heads], axis=0
        )
        query = jnp.concatenate([query, unit], axis=1)
        scores[pair % 2] = lax.dot_general(
            k_ref[...], query, (((1,), (1,)), ((), ())),
            preferred_element_type=jnp.float32,
        )

    load_q.wait()
    load_k.wait()
    score(0)
    load_v.wait()
    vt_ref[:HD] = v_ref[...].T
    vt_ref[HD:] = jnp.ones((ONE_ROWS, keys), jnp.bfloat16)
    for pair in range(pairs):
        if pair + 1 < pairs:
            score(pair + 1)
        block = scores[pair % 2]
        peak = jnp.max(block, axis=0, keepdims=True)
        weights = jnp.exp2((block - peak) * (SCALE * LOG2E)).astype(jnp.bfloat16)
        outs = jnp.dot(vt_ref[...], weights, preferred_element_type=jnp.float32)
        total = outs[HD : HD + 1]
        stat = peak * SCALE + jnp.log(total)
        outs = (outs[:HD] * (1.0 / total)).astype(jnp.bfloat16)
        if pair == 0:
            pl.semaphore_wait(barrier, 2 * (n - 1) + nk - 1)
        for kind in range(2):
            here = slice(kind * rows, (kind + 1) * rows)
            place = orders[kind][pair]
            stat0[kind, place] = stat[:, here]
            for half in range(2):
                owner = place * 2 + half
                send1[kind, owner] = outs[half * HALF : (half + 1) * HALF, here]
                if pair + 1 < pairs:
                    give(kind, place, owner)
            if pair + 1 == pairs:
                own = mine[kind]
                give(kind, place, own + 1 - 2 * lax.rem(own, 2))
                recv1[kind, own] = send1[kind, own]
                stat1[kind, own] = stat[:, here]

    load_w.wait()
    wt_ref[...] = w_ref[...].T

    for kind in range(2):
        take(recv1.at[kind, pl.ds(0, n - 1)], recv_sem.at[kind])
        take(stat1.at[kind, pl.ds(0, n - 1)], recv_sem.at[7 + kind])
        merged, stat = merge_slots(recv1.at[kind], stat1.at[kind])
        across = mine[1 - kind]
        slot = recv2.at[kind, across]
        slot[...] = merged.astype(jnp.bfloat16)
        stat2[kind, across] = stat
        for step in far_first(n):
            to = lax.rem(across + step, n)
            send(slot, slot, 2 + kind, along(1 - kind, to))
            row = stat2.at[kind, across]
            send(row, row, 9 + kind, along(1 - kind, to))

    for kind in range(2):
        take(recv2.at[kind, pl.ds(0, n - 1)], recv_sem.at[2 + kind])
        take(stat2.at[kind, pl.ds(0, n - 1)], recv_sem.at[9 + kind])
        merged, _ = merge_slots(recv2.at[kind], stat2.at[kind])
        slot = att.at[kind, mine[kind]]
        slot[...] = merged.astype(jnp.bfloat16)
        for step in far_first(n):
            to = lax.rem(mine[kind] + step, n)
            send(slot, slot, 4 + kind, along(kind, to))

    mixed = None
    for kind in range(2):
        take(att.at[kind, pl.ds(0, n - 1)], recv_sem.at[4 + kind])
        part = jnp.dot(
            wt_ref[:, kind * n * HALF : (kind + 1) * n * HALF],
            att[kind].reshape(n * HALF, rows),
            preferred_element_type=jnp.float32,
        )
        mixed = part if mixed is None else mixed + part
    send3[...] = mixed.T.reshape(send3.shape)
    for step in far_first(nk):
        to = lax.rem(kvh + step, nk)
        send(send3.at[to], recv3.at[kvh], 6, on_kvh(step))
    recv3[kvh] = send3[kvh]
    take(recv3.at[pl.ds(0, nk - 1)], recv_sem.at[6])
    out_ref[...] = jnp.sum(recv3[...], axis=0).astype(jnp.bfloat16)

    for kind in range(2):
        take(send1.at[kind, pl.ds(0, n - 1)], send_sem.at[kind])
        take(stat1.at[kind, pl.ds(0, n - 1)], send_sem.at[7 + kind])
        take(recv2.at[kind, pl.ds(0, n - 1)], send_sem.at[2 + kind])
        take(stat2.at[kind, pl.ds(0, n - 1)], send_sem.at[9 + kind])
        take(att.at[kind, pl.ds(0, n - 1)], send_sem.at[4 + kind])
    take(send3.at[pl.ds(0, nk - 1)], send_sem.at[6])


def solution(mesh):
    nk = mesh.shape["kvh"]
    n = math.isqrt(mesh.shape["ctx"])

    def step(queries, cache_keys, cache_values, lengths, w_out):
        rows, keys = queries.shape[0], cache_keys.shape[0]
        bf16, f32 = jnp.bfloat16, jnp.float32
        in_hbm = pl.BlockSpec(memory_space=pltpu.HBM)
        return pl.pallas_call(
            functools.partial(kernel, nk, n),
            out_shape=jax.ShapeDtypeStruct((rows // nk, HD), bf16),
            in_specs=[in_hbm] * 5,
            out_specs=pl.BlockSpec(memory_space=pltpu.VMEM),
            scratch_shapes=[
                pltpu.SMEM((1,), jnp.int32),
                pltpu.VMEM(queries.shape, bf16),
                pltpu.VMEM((keys, 2 * HD), bf16),
                pltpu.VMEM((keys, HD), bf16),
                pltpu.VMEM(w_out.shape, bf16),
                pltpu.VMEM((HD + ONE_ROWS, keys), bf16),
                pltpu.VMEM((HD, n * HD), bf16),
                pltpu.VMEM((2, keys, 2 * rows), f32),
                pltpu.VMEM((2, n, HALF, rows), bf16),
                pltpu.VMEM((2, n, HALF, rows), bf16),
                pltpu.VMEM((2, n, HALF, rows), bf16),
                pltpu.VMEM((2, n // 2, 1, rows), f32),
                pltpu.VMEM((2, n, 1, rows), f32),
                pltpu.VMEM((2, n, 1, rows), f32),
                pltpu.VMEM((2, n, HALF, rows), bf16),
                pltpu.VMEM((nk, rows // nk, HD), f32),
                pltpu.VMEM((nk, rows // nk, HD), f32),
                pltpu.SemaphoreType.DMA((5,)),
                pltpu.SemaphoreType.DMA((11,)),
                pltpu.SemaphoreType.DMA((11,)),
            ],
            compiler_params=pltpu.CompilerParams(
                collective_id=0, has_side_effects=True, vmem_limit_bytes=VMEM_BYTES
            ),
        )(lengths, queries, cache_keys, cache_values, w_out)

    in_specs = (P(None, "kvh"), P("ctx", "kvh"), P("ctx", "kvh"), P("ctx"), P("kvh", "ctx"))
    out_specs = P("kvh", "ctx")
    return jax.shard_map(step, mesh=mesh, in_specs=in_specs, out_specs=out_specs, check_vma=False)
```

time: 356 us -> 37.3 us (0.10)
  blocking collectives: 234 us -> 0 us
  waiting for transfers between devices: 97.4 us -> 0 us
  Pallas kernels: 0 us -> 35.9 us
  between operations: 14.2 us -> 0.66 us
  other arithmetic: 4.09 us -> 0 us
  matrix products: 3.77 us -> 0 us
    pmax x1 -> x0, blocking collectives: 123 us -> none  [shards(): joined = lax.pmax(maxima, 'ctx')]
    psum x1 -> x0, blocking collectives: 110 us -> none  [shards(): lax.psum((totals * factor, outputs * factor.T[:, :, None]), 'ctx')]
    psum x1 -> x0, waiting for transfers between devices: 62 us -> none  [shards(): lax.psum((totals * factor, outputs * factor.T[:, :, None]), 'ctx')]
    pallas_call x0 -> x1, Pallas kernels: none -> 35.9 us  [step(): pl.pallas_call(functools.partial(kernel, nk, n), out_shape=jax.ShapeDtype...]
    reduce_scatter x1 -> x0, waiting for transfers between devices: 35.3 us -> none  [shards(): lax.psum_scatter(jnp.dot(attended, w_out, preferred_element_type=jnp.floa...]
    dot_general x5 -> x0, matrix products: 3.77 us -> none  [the longest x2 1.67 us: local_partials(): jnp.einsum('hqk,kd->qhd', weights.astype(jnp.bfloat16), cache_values, pre...]
  transfers between devices with their start and end apart: 2 -> 0, of which waited for: 2 -> 0; matrix products, arithmetic and copies ran while one was open for 0% -> 0% of each run, Pallas kernels for 0% -> 0%
where the time goes in v2:
time: 37.3 us; the launch traced here: 37.2 us
  Pallas kernels  35.9 us (96%)
  between operations  0.66 us (2%)
  local copies, waits for them, and re-layouts  0.6 us (2%)
    pallas_call x1, Pallas kernels, step(): pl.pallas_call(functools.partial(kernel, nk, n), out_shape=jax.ShapeDtype...  35.9 us

profile of v2, /device:TPU:1, one launch (start us, length us, event | category | flops | bytes accessed | tf_op | source)
XLA Modules:
  0.0 37.2 jit_solution(1371306580085881250)
XLA Ops:
  0.7 35.9 %shard_map.55 = bf16[16,128]{1,0:T(8,128)(2,1)S(1)} custom-call(s32[1]{0:T(128)S(6)} %copy.7.len_hbm, bf16[128,1024]{1,0:T(8,128)(2,1)} %q_hbm.1, bf16[1024,128]{1,0:T(8,128)(2,1)} %k_hbm.1, bf16[1024,128]{1,0:T(8,128)(2,1)} %v_hbm.1, bf16[1024,128]{1,0:T(8,128)(2,1)} %w_hbm.1), custom_call_target="tpu_custom_call" | custom-call | tf_op jit(solution)/shard_map/pallas_call | solution.py:216
  36.6 0.6 %copy.8 = bf16[16,128]{1,0:T(8,128)(2,1)} copy(bf16[16,128]{1,0:T(8,128)(2,1)S(1)} %shard_map.55) | data formatting | bytes 8192

commit v3 on v2

--- a/solution.py
+++ b/solution.py
@@ -18,32 +18,30 @@
 MESH = pl.DeviceIdType.MESH
 
 
-def merge(parts, stats):
-    top = functools.reduce(jnp.maximum, stats)
-    shares = [jnp.exp(stat - top) for stat in stats]
+def shares_of(stats):
+    rows = [stats[j] for j in range(stats.shape[0])]
+    top = functools.reduce(jnp.maximum, rows)
+    shares = [jnp.exp(row - top) for row in rows]
     total = functools.reduce(jnp.add, shares)
     scale = 1.0 / total
-    merged = functools.reduce(
-        jnp.add, [part * (share * scale) for part, share in zip(parts, shares)]
-    )
-    return merged, top + jnp.log(total)
+    return [share * scale for share in shares], top + jnp.log(total)
+
+
+def merge(slots, shares):
+    return functools.reduce(
+        jnp.add,
+        [slots[j].astype(jnp.float32) * share for j, share in enumerate(shares)],
+    ).astype(jnp.bfloat16)
 
 
 def far_first(n):
     return sorted(range(1, n), key=lambda step: -min(step, n - step))
 
 
-def merge_slots(slots, stats):
-    n = slots.shape[0]
-    return merge(
-        [slots[j].astype(jnp.float32) for j in range(n)], [stats[j] for j in range(n)]
-    )
-
-
 def kernel(
     nk, n,
-    len_hbm, q_hbm, k_hbm, v_hbm, w_hbm, out_ref,
-    len_ref, q_ref, k_ref, v_ref, w_ref, vt_ref, wt_ref, scores,
+    len_ref, q_hbm, k_hbm, v_hbm, w_hbm, out_ref,
+    q_ref, k_ref, v_ref, w_ref, vt_ref, wt_ref, scores,
     send1, recv1, recv2, stat0, stat1, stat2, att, send3, recv3,
     load_sem, send_sem, recv_sem,
 ):
@@ -57,12 +55,10 @@
 
     load_k = pltpu.make_async_copy(k_hbm, k_ref.at[:, pl.ds(0, HD)], load_sem.at[0])
     load_q = pltpu.make_async_copy(q_hbm, q_ref, load_sem.at[1])
-    load_len = pltpu.make_async_copy(len_hbm, len_ref, load_sem.at[2])
-    load_v = pltpu.make_async_copy(v_hbm, v_ref, load_sem.at[3])
-    load_w = pltpu.make_async_copy(w_hbm, w_ref, load_sem.at[4])
+    load_v = pltpu.make_async_copy(v_hbm, v_ref, load_sem.at[2])
+    load_w = pltpu.make_async_copy(w_hbm, w_ref, load_sem.at[3])
     load_k.start()
     load_q.start()
-    load_len.start()
 
     def along(kind, to):
         return (kvh, to * n + z) if kind == 0 else (kvh, y * n + to)
@@ -94,7 +90,6 @@
     unit = jnp.where(lane == 0, 1.0, 0.0).astype(jnp.bfloat16)
     position = lax.broadcasted_iota(jnp.int32, (keys, HD), 0)
     column = lax.broadcasted_iota(jnp.int32, (keys, HD), 1)
-    load_len.wait()
     bias = jnp.where((column == 0) & (position >= len_ref[0]), MASKED, 0.0)
     k_ref[:, HD:] = bias.astype(jnp.bfloat16)
 
@@ -105,8 +100,8 @@
 
     def give(kind, place, owner):
         device = along(kind, owner)
+        send(stat0.at[kind, place], stat1.at[kind, mine[kind]], 7 + kind, device)
         send(send1.at[kind, owner], recv1.at[kind, mine[kind]], kind, device)
-        send(stat0.at[kind, place], stat1.at[kind, mine[kind]], 7 + kind, device)
 
     def score(pair):
         heads = [orders[kind][pair] + kind * pairs for kind in range(2)]
@@ -156,28 +151,27 @@
     wt_ref[...] = w_ref[...].T
 
     for kind in range(2):
+        take(stat1.at[kind, pl.ds(0, n - 1)], recv_sem.at[7 + kind])
+        shares, stat = shares_of(stat1.at[kind])
+        across = mine[1 - kind]
+        row, slot = stat2.at[kind, across], recv2.at[kind, across]
+        row[...] = stat
         take(recv1.at[kind, pl.ds(0, n - 1)], recv_sem.at[kind])
-        take(stat1.at[kind, pl.ds(0, n - 1)], recv_sem.at[7 + kind])
-        merged, stat = merge_slots(recv1.at[kind], stat1.at[kind])
-        across = mine[1 - kind]
-        slot = recv2.at[kind, across]
-        slot[...] = merged.astype(jnp.bfloat16)
-        stat2[kind, across] = stat
+        slot[...] = merge(recv1.at[kind], shares)
         for step in far_first(n):
-            to = lax.rem(across + step, n)
-            send(slot, slot, 2 + kind, along(1 - kind, to))
-            row = stat2.at[kind, across]
-            send(row, row, 9 + kind, along(1 - kind, to))
-
-    for kind in range(2):
+            device = along(1 - kind, lax.rem(across + step, n))
+            send(row, row, 9 + kind, device)
+            send(slot, slot, 2 + kind, device)
+
+    for kind in range(2):
+        take(stat2.at[kind, pl.ds(0, n - 1)], recv_sem.at[9 + kind])
+        shares, _ = shares_of(stat2.at[kind])
+        slot = att.at[kind, mine[kind]]
         take(recv2.at[kind, pl.ds(0, n - 1)], recv_sem.at[2 + kind])
-        take(stat2.at[kind, pl.ds(0, n - 1)], recv_sem.at[9 + kind])
-        merged, _ = merge_slots(recv2.at[kind], stat2.at[kind])
-        slot = att.at[kind, mine[kind]]
-        slot[...] = merged.astype(jnp.bfloat16)
+        slot[...] = merge(recv2.at[kind], shares)
         for step in far_first(n):
-            to = lax.rem(mine[kind] + step, n)
-            send(slot, slot, 4 + kind, along(kind, to))
+            device = along(kind, lax.rem(mine[kind] + step, n))
+            send(slot, slot, 4 + kind, device)
 
     mixed = None
     for kind in range(2):
@@ -193,8 +187,6 @@
         to = lax.rem(kvh + step, nk)
         send(send3.at[to], recv3.at[kvh], 6, on_kvh(step))
     recv3[kvh] = send3[kvh]
-    take(recv3.at[pl.ds(0, nk - 1)], recv_sem.at[6])
-    out_ref[...] = jnp.sum(recv3[...], axis=0).astype(jnp.bfloat16)
 
     for kind in range(2):
         take(send1.at[kind, pl.ds(0, n - 1)], send_sem.at[kind])
@@ -202,6 +194,9 @@
         take(recv2.at[kind, pl.ds(0, n - 1)], send_sem.at[2 + kind])
         take(stat2.at[kind, pl.ds(0, n - 1)], send_sem.at[9 + kind])
         take(att.at[kind, pl.ds(0, n - 1)], send_sem.at[4 + kind])
+
+    take(recv3.at[pl.ds(0, nk - 1)], recv_sem.at[6])
+    out_ref[...] = jnp.sum(recv3[...], axis=0).astype(jnp.bfloat16)
     take(send3.at[pl.ds(0, nk - 1)], send_sem.at[6])
 
 
@@ -216,10 +211,9 @@
         return pl.pallas_call(
             functools.partial(kernel, nk, n),
             out_shape=jax.ShapeDtypeStruct((rows // nk, HD), bf16),
-            in_specs=[in_hbm] * 5,
+            in_specs=[pl.BlockSpec(memory_space=pltpu.SMEM)] + [in_hbm] * 4,
             out_specs=pl.BlockSpec(memory_space=pltpu.VMEM),
             scratch_shapes=[
-                pltpu.SMEM((1,), jnp.int32),
                 pltpu.VMEM(queries.shape, bf16),
                 pltpu.VMEM((keys, 2 * HD), bf16),
                 pltpu.VMEM((keys, HD), bf16),
@@ -236,7 +230,7 @@
                 pltpu.VMEM((2, n, HALF, rows), bf16),
                 pltpu.VMEM((nk, rows // nk, HD), f32),
                 pltpu.VMEM((nk, rows // nk, HD), f32),
-                pltpu.SemaphoreType.DMA((5,)),
+                pltpu.SemaphoreType.DMA((4,)),
                 pltpu.SemaphoreType.DMA((11,)),
                 pltpu.SemaphoreType.DMA((11,)),
             ],

time: 37.3 us -> 37.2 us (level)
  no operation moved by 1% of the time
where the time goes in v3:
time: 37.2 us; the launch traced here: 37 us
  Pallas kernels  35.8 us (96%)
  between operations  0.66 us (2%)
  local copies, waits for them, and re-layouts  0.6 us (2%)
    pallas_call x1, Pallas kernels, step(): pl.pallas_call(functools.partial(kernel, nk, n), out_shape=jax.ShapeDtype...  35.8 us

profile of v3, /device:TPU:1, one launch (start us, length us, event | category | flops | bytes accessed | tf_op | source)
XLA Modules:
  0.0 37.0 jit_solution(3710717179568797289)
XLA Ops:
  0.7 35.8 %shard_map.55 = bf16[16,128]{1,0:T(8,128)(2,1)S(1)} custom-call(s32[1]{0:T(128)S(6)} %copy.7.len_ref, bf16[128,1024]{1,0:T(8,128)(2,1)} %q_hbm.1, bf16[1024,128]{1,0:T(8,128)(2,1)} %k_hbm.1, bf16[1024,128]{1,0:T(8,128)(2,1)} %v_hbm.1, bf16[1024,128]{1,0:T(8,128)(2,1)} %w_hbm.1), custom_call_target="tpu_custom_call" | custom-call | tf_op jit(solution)/shard_map/pallas_call | solution.py:211
  36.4 0.6 %copy.8 = bf16[16,128]{1,0:T(8,128)(2,1)} copy(bf16[16,128]{1,0:T(8,128)(2,1)S(1)} %shard_map.55) | data formatting | bytes 8192

commit v4 on v3

--- a/solution.py
+++ b/solution.py
@@ -59,6 +59,8 @@
     load_w = pltpu.make_async_copy(w_hbm, w_ref, load_sem.at[3])
     load_k.start()
     load_q.start()
+    load_v.start()
+    load_w.start()
 
     def along(kind, to):
         return (kvh, to * n + z) if kind == 0 else (kvh, y * n + to)
@@ -74,9 +76,6 @@
     for step in range(1, nk):
         pl.semaphore_signal(barrier, inc=1, device_id=on_kvh(step), device_id_type=MESH)
 
-    load_v.start()
-    load_w.start()
-
     def send(src, dst, index, device):
         pltpu.make_async_remote_copy(
             src_ref=src, dst_ref=dst, send_sem=send_sem.at[index],
@@ -93,10 +92,13 @@
     bias = jnp.where((column == 0) & (position >= len_ref[0]), MASKED, 0.0)
     k_ref[:, HD:] = bias.astype(jnp.bfloat16)
 
-    orders = [
-        [lax.rem(mine[kind] // 2 + step, pairs) for step in far_first(pairs) + [0]]
-        for kind in range(2)
-    ]
+    orders = []
+    for kind in range(2):
+        place, odd = mine[kind] // 2, lax.rem(mine[kind], 2)
+        steps = far_first(pairs) + [0]
+        if pairs == 4:
+            steps = [2, 1 + 2 * odd, 3 - 2 * odd, 0]
+        orders.append([lax.rem(place + step, pairs) for step in steps])
 
     def give(kind, place, owner):
         device = along(kind, owner)

time: 37.2 us -> 36.9 us (level)
  no operation moved by 1% of the time
where the time goes in v4:
time: 36.9 us; the launch traced here: 36.8 us
  Pallas kernels  35.5 us (96%)
  between operations  0.66 us (2%)
  local copies, waits for them, and re-layouts  0.6 us (2%)
    pallas_call x1, Pallas kernels, step(): pl.pallas_call(functools.partial(kernel, nk, n), out_shape=jax.ShapeDtype...  35.5 us

profile of v4, /device:TPU:1, one launch (start us, length us, event | category | flops | bytes accessed | tf_op | source)
XLA Modules:
  0.0 36.8 jit_solution(15044867683051761896)
XLA Ops:
  0.7 35.5 %shard_map.55 = bf16[16,128]{1,0:T(8,128)(2,1)S(1)} custom-call(s32[1]{0:T(128)S(6)} %copy.7.len_ref, bf16[128,1024]{1,0:T(8,128)(2,1)} %q_hbm.1, bf16[1024,128]{1,0:T(8,128)(2,1)} %k_hbm.1, bf16[1024,128]{1,0:T(8,128)(2,1)} %v_hbm.1, bf16[1024,128]{1,0:T(8,128)(2,1)} %w_hbm.1), custom_call_target="tpu_custom_call" | custom-call | tf_op jit(solution)/shard_map/pallas_call | solution.py:213
  36.2 0.6 %copy.8 = bf16[16,128]{1,0:T(8,128)(2,1)} copy(bf16[16,128]{1,0:T(8,128)(2,1)S(1)} %shard_map.55) | data formatting | bytes 8192

commit v5 on v4

--- a/solution.py
+++ b/solution.py
@@ -165,7 +165,7 @@
             send(row, row, 9 + kind, device)
             send(slot, slot, 2 + kind, device)
 
-    for kind in range(2):
+    for kind in (1, 0):
         take(stat2.at[kind, pl.ds(0, n - 1)], recv_sem.at[9 + kind])
         shares, _ = shares_of(stat2.at[kind])
         slot = att.at[kind, mine[kind]]
@@ -176,7 +176,7 @@
             send(slot, slot, 4 + kind, device)
 
     mixed = None
-    for kind in range(2):
+    for kind in (1, 0):
         take(att.at[kind, pl.ds(0, n - 1)], recv_sem.at[4 + kind])
         part = jnp.dot(
             wt_ref[:, kind * n * HALF : (kind + 1) * n * HALF],

time: 36.9 us -> 36.8 us (level)
  no operation moved by 1% of the time
where the time goes in v5:
time: 36.8 us; the launch traced here: 36.7 us
  Pallas kernels  35.4 us (96%)
  between operations  0.66 us (2%)
  local copies, waits for them, and re-layouts  0.6 us (2%)
    pallas_call x1, Pallas kernels, step(): pl.pallas_call(functools.partial(kernel, nk, n), out_shape=jax.ShapeDtype...  35.4 us

profile of v5, /device:TPU:1, one launch (start us, length us, event | category | flops | bytes accessed | tf_op | source)
XLA Modules:
  0.0 36.7 jit_solution(3957237395203353877)
XLA Ops:
  0.7 35.4 %shard_map.55 = bf16[16,128]{1,0:T(8,128)(2,1)S(1)} custom-call(s32[1]{0:T(128)S(6)} %copy.7.len_ref, bf16[128,1024]{1,0:T(8,128)(2,1)} %q_hbm.1, bf16[1024,128]{1,0:T(8,128)(2,1)} %k_hbm.1, bf16[1024,128]{1,0:T(8,128)(2,1)} %v_hbm.1, bf16[1024,128]{1,0:T(8,128)(2,1)} %w_hbm.1), custom_call_target="tpu_custom_call" | custom-call | tf_op jit(solution)/shard_map/pallas_call | solution.py:213
  36.1 0.6 %copy.8 = bf16[16,128]{1,0:T(8,128)(2,1)} copy(bf16[16,128]{1,0:T(8,128)(2,1)S(1)} %shard_map.55) | data formatting | bytes 8192

commit v6 on v5

--- a/solution.py
+++ b/solution.py
@@ -35,7 +35,7 @@
 
 
 def far_first(n):
-    return sorted(range(1, n), key=lambda step: -min(step, n - step))
+    return sorted(range(n - 1, 0, -1), key=lambda step: -min(step, n - step))
 
 
 def kernel(

time: 36.8 us -> 36.8 us (level)
  no operation moved by 1% of the time
where the time goes in v6:
time: 36.8 us; the launch traced here: 36.7 us
  Pallas kernels  35.5 us (96%)
  between operations  0.66 us (2%)
  local copies, waits for them, and re-layouts  0.6 us (2%)
    pallas_call x1, Pallas kernels, step(): pl.pallas_call(functools.partial(kernel, nk, n), out_shape=jax.ShapeDtype...  35.5 us

profile of v6, /device:TPU:1, one launch (start us, length us, event | category | flops | bytes accessed | tf_op | source)
XLA Modules:
  0.0 36.7 jit_solution(9050234206666207143)
XLA Ops:
  0.7 35.5 %shard_map.55 = bf16[16,128]{1,0:T(8,128)(2,1)S(1)} custom-call(s32[1]{0:T(128)S(6)} %copy.7.len_ref, bf16[128,1024]{1,0:T(8,128)(2,1)} %q_hbm.1, bf16[1024,128]{1,0:T(8,128)(2,1)} %k_hbm.1, bf16[1024,128]{1,0:T(8,128)(2,1)} %v_hbm.1, bf16[1024,128]{1,0:T(8,128)(2,1)} %w_hbm.1), custom_call_target="tpu_custom_call" | custom-call | tf_op jit(solution)/shard_map/pallas_call | solution.py:213
  36.1 0.6 %copy.8 = bf16[16,128]{1,0:T(8,128)(2,1)} copy(bf16[16,128]{1,0:T(8,128)(2,1)S(1)} %shard_map.55) | data formatting | bytes 8192
